TPU v7x, 1024 devices: a whole 8x8x8 slice. The times are simulated.
1024 devices in a mesh: src: 32 (over y_lo, x), rec: 8 (over z), freq: 4 (over y_hi, core).
Axes of the slice: x: 8, y: 8 (y_hi: 2, y_lo: 4; y = y_hi * 4 + y_lo), z: 8, core: 2. Of those that a mesh axis runs over, the one named last changes fastest.
Arguments:
- wave: bfloat16 [2, 8, 2048, 4096], P(None, 'freq', 'src', 'rec'), may hold values from -6 to 6
- tap_table: float32 [2, 64, 8, 33], P(None, None, 'freq'), may hold values from -0.75 to 0.75
- src_index: int32 [3, 2048], P(None, 'src'), may hold values from 0 to 63
- rec_index: int32 [3, 4096], P(None, 'rec'), may hold values from 0 to 63
- offset_bin: int32 [2048, 4096], P('src', 'rec'), may hold values from 0 to 63
- bin_weight: float32 [3, 64], replicated, may hold values from 0.5 to 2
Outputs:
- final_wave: bfloat16 [2, 8, 2048, 4096], P(None, 'freq', 'src', 'rec')
- image: float32 [2048, 4096], P(('src', 'freq'), 'rec')
All inputs are finite; a program needn't handle non-finite values.
Results may differ from a plain program's by a relative error of at most 0.012.
Values may be sent and summed in bfloat16 or wider, within the bound.
A program may use at most 32 MiB of HBM per device.

v0:
```python
import math

import jax
import jax.numpy as jnp
from jax import lax
from jax.sharding import PartitionSpec as P

TAPS = 33
DEPTHS = 3


def padded_2(cells, sides, width):
    for axis, dim in sides:
        count = lax.axis_size(axis)
        ends = count - 1
        head = lax.slice_in_dim(cells, 0, width, axis=dim)
        tail = lax.slice_in_dim(cells, cells.shape[dim] - width, cells.shape[dim], axis=dim)
        cells = jnp.concatenate(
            [
                lax.ppermute(tail, axis, [(i, (i + 1) % count) for i in range(ends)]),
                cells,
                lax.ppermute(head, axis, [((i + 1) % count, i) for i in range(ends)]),
            ],
            axis=dim,
        )
    return cells


def banded(tap_rows, block_size):
    leading = tap_rows.shape[:-2]
    tap_count = tap_rows.shape[-1]
    block_count = tap_rows.shape[-2] // block_size
    grouped = tap_rows.reshape(leading + (block_count, block_size, tap_count))
    padded = jnp.pad(grouped, [(0, 0)] * (len(leading) + 2) + [(0, block_size)])
    flattened = padded.reshape(leading + (block_count, block_size * (tap_count + block_size)))
    flattened = flattened[..., : block_size * (block_size + tap_count - 1)]
    return flattened.reshape(leading + (block_count, block_size, block_size + tap_count - 1))


def operator_pair(tap_rows, block_size):
    matrices = banded(tap_rows, block_size)
    real_part = jnp.concatenate([matrices[0], -matrices[1]], axis=-1)
    imag_part = jnp.concatenate([matrices[1], matrices[0]], axis=-1)
    return (real_part, imag_part)


def position_taps(table_bf, index_row):
    onehot = (index_row[:, None] == jnp.arange(table_bf.shape[1], dtype=jnp.int32)).astype(
        jnp.bfloat16
    )
    gathered = jnp.einsum("ln,cnfk->cflk", onehot, table_bf, preferred_element_type=jnp.float32)
    return gathered.astype(jnp.bfloat16)


def pair_weights(offset_bin, bin_weight):
    row_count, col_count = offset_bin.shape
    bin_count = bin_weight.shape[1]
    grouped = offset_bin.reshape(row_count // 8, 8, col_count)

    def one_block(bins_block):
        onehot = (bins_block[:, :, None] == jnp.arange(bin_count, dtype=jnp.int32)).astype(
            jnp.float32
        )
        return jnp.einsum("srh,zh->zsr", onehot, bin_weight, precision=lax.Precision.HIGHEST)

    blocks = lax.map(one_block, grouped)
    return jnp.moveaxis(blocks, 1, 0).reshape(bin_weight.shape[0], row_count, col_count)


def receiver_pass(padded, operators, block_size):
    block_count = operators[0].shape[1]
    extra = (block_count + 1) * block_size - padded.shape[3]
    widened = jnp.pad(padded, ((0, 0), (0, 0), (0, 0), (0, extra)))
    grouped = widened.reshape(padded.shape[:3] + (block_count + 1, block_size))
    windows = jnp.concatenate(
        [grouped[..., :block_count, :], grouped[..., 1:, : TAPS - 1]], axis=-1
    )
    stacked = jnp.concatenate([windows[0], windows[1]], axis=-1)
    real_out = jnp.einsum(
        "fsnj,fncj->fsnc", stacked, operators[0], preferred_element_type=jnp.float32
    )
    imag_out = jnp.einsum(
        "fsnj,fncj->fsnc", stacked, operators[1], preferred_element_type=jnp.float32
    )
    result = jnp.stack([real_out, imag_out]).reshape(padded.shape[:3] + (block_count * block_size,))
    return result.astype(jnp.bfloat16)


def source_pass(padded, operators, block_size):
    block_count = operators[0].shape[1]
    extra = (block_count + 1) * block_size - padded.shape[2]
    widened = jnp.pad(padded, ((0, 0), (0, 0), (0, extra), (0, 0)))
    grouped = widened.reshape(padded.shape[:2] + (block_count + 1, block_size, padded.shape[3]))
    windows = jnp.concatenate([grouped[:, :, :block_count], grouped[:, :, 1:, : TAPS - 1]], axis=3)
    stacked = jnp.concatenate([windows[0], windows[1]], axis=2)
    real_out = jnp.einsum(
        "fnjr,fncj->fncr", stacked, operators[0], preferred_element_type=jnp.float32
    )
    imag_out = jnp.einsum(
        "fnjr,fncj->fncr", stacked, operators[1], preferred_element_type=jnp.float32
    )
    result = jnp.stack([real_out, imag_out]).reshape(
        padded.shape[:2] + (block_count * block_size, padded.shape[3])
    )
    return result.astype(jnp.bfloat16)


def shards(wave, tap_table, src_index, rec_index, offset_bin, bin_weight):
    half_taps = TAPS // 2
    row_count = wave.shape[2]
    col_count = wave.shape[3]
    block_src = min(128, row_count)
    block_rec = min(128, col_count)
    table_bf = tap_table.astype(jnp.bfloat16)
    pair_weight = pair_weights(offset_bin, bin_weight)
    wavefield = wave
    image_part = jnp.zeros((row_count, col_count), jnp.float32)
    for depth_step in range(DEPTHS):
        rec_ops = operator_pair(position_taps(table_bf, rec_index[depth_step]), block_rec)
        src_ops = operator_pair(position_taps(table_bf, src_index[depth_step]), block_src)
        framed = padded_2(wavefield, (("rec", 3),), half_taps)
        swept = padded_2(receiver_pass(framed, rec_ops, block_rec), (("src", 2),), half_taps)
        wavefield = source_pass(swept, src_ops, block_src)
        image_part = image_part + pair_weight[depth_step] * jnp.sum(
            wavefield[0].astype(jnp.float32), axis=0
        )
    total = lax.psum_scatter(
        image_part.astype(jnp.bfloat16), "freq", scatter_dimension=0, tiled=True
    ).astype(jnp.float32)
    scale = 1.0 / math.sqrt(wave.shape[1] * lax.axis_size("freq") * DEPTHS)
    return (wavefield, total * scale)


def solution(mesh):
    placed = (
        P(None, "freq", "src", "rec"),
        P(None, None, "freq", None),
        P(None, "src"),
        P(None, "rec"),
        P("src", "rec"),
        P(),
    )
    return jax.shard_map(
        shards,
        mesh=mesh,
        in_specs=placed,
        out_specs=(P(None, "freq", "src", "rec"), P(("src", "freq"), "rec")),
        check_vma=False,
    )
```

profile of v0, /device:TPU:1, one launch (start us, length us, event | category | flops | bytes accessed | tf_op | source)
XLA Modules:
  0.0 168.1 jit_solution(4050683803212149814)
XLA Ops:
  7.2 1.6 fusion.138
  8.8 6.3 %collective-permute-start = (bf16[2,2,64,16]{3,2,1,0:T(8,128)(2,1)}, bf16[2,2,64,16]{3,2,1,0:T(8,128)(2,1)}, u32[]{:S(2)}, u32[]{:S(2)}) collective-permute-start(bf16[2,2,64,16]{3,2,1,0:T(8,128)(2,1)} %get-tuple-element.64), channel_id=1, source_target_pairs={{0,4},{4,8},{8,12},{12,16},{16,20},{20,24},{24,28},{1,5},{5,9},{9,... | collective-permute-start | bytes 24584 | tf_op jit(solution)/shard_map/ppermute | solution.py:20
  15.1 1.3 collective-permute-start.1
  18.9 1.6 reshape.234
  22.7 1.6 reshape.229
  25.2 1.6 reshape.224
  27.5 14.2 %while.10 = (s32[]{:T(128)}, f32[8,3,8,512]{3,1,2,0:T(4,128)}, s32[8,8,512]{2,1,0:T(8,128)}, f32[3,64]{1,0:T(4,128)S(1)}, s32[]{:T(128)}) while((s32[]{:T(128)}, f32[8,3,8,512]{3,1,2,0:T(4,128)}, s32[8,8,512]{2,1,0:T(8,128)}, f32[3,64]{1,0:T(4,128)S(1)}, s32[]{:T(128)}) %tuple.55), condition=%wide.region_1.2_spmd, body=%wide.region_0.1_spmd.sunk | while | flops 9699330 | bytes 116033 | solution.py:66
  48.8 3.1 %collective-permute-start.2 = (bf16[2,2,16,512]{3,2,1,0:T(8,128)(2,1)S(1)}, bf16[2,2,16,512]{3,2,1,0:T(8,128)(2,1)S(1)}, u32[]{:S(2)}, u32[]{:S(2)}) collective-permute-start(bf16[2,2,16,512]{3,2,1,0:T(8,128)(2,1)S(1)} %get-tuple-element.62), channel_id=1, source_target_pairs={{0,32},{32,64},{64,96},{96,128},{128,160},{160,192},{192,224},{224... | collective-permute-start | bytes 196616 | tf_op jit(solution)/shard_map/ppermute | solution.py:20
  51.9 1.5 collective-permute-start.3
  54.0 2.9 %collective-permute-done.3 = bf16[2,2,16,512]{3,2,1,0:T(8,128)(2,1)S(1)} collective-permute-done((bf16[2,2,16,512]{3,2,1,0:T(8,128)(2,1)S(1)}, bf16[2,2,16,512]{3,2,1,0:T(8,128)(2,1)S(1)}, u32[]{:S(2)}, u32[]{:S(2)}) %collective-permute-start.3) | collective-permute-done | bytes 65568 | tf_op jit(solution)/shard_map/ppermute | solution.py:22
  58.1 4.9 %collective-permute-start.4 = (bf16[2,2,64,16]{3,2,1,0:T(8,128)(2,1)S(1)}, bf16[2,2,64,16]{3,2,1,0:T(8,128)(2,1)S(1)}, u32[]{:S(2)}, u32[]{:S(2)}) collective-permute-start(bf16[2,2,64,16]{3,2,1,0:T(8,128)(2,1)S(1)} %get-tuple-element.60), channel_id=1, source_target_pairs={{0,4},{4,8},{8,12},{12,16},{16,20},{20,24},{24,28},{1,5},{5,9},{9,... | collective-permute-start | bytes 24584 | tf_op jit(solution)/shard_map/ppermute | solution.py:20
  63.0 1.3 collective-permute-start.5
  66.5 3.1 %collective-permute-done.5 = bf16[2,2,64,16]{3,2,1,0:T(8,128)(2,1)S(1)} collective-permute-done((bf16[2,2,64,16]{3,2,1,0:T(8,128)(2,1)S(1)}, bf16[2,2,64,16]{3,2,1,0:T(8,128)(2,1)S(1)}, u32[]{:S(2)}, u32[]{:S(2)}) %collective-permute-start.5) | collective-permute-done | bytes 8224 | tf_op jit(solution)/shard_map/ppermute | solution.py:22
  71.7 3.1 %collective-permute-start.6 = (bf16[2,2,16,512]{3,2,1,0:T(8,128)(2,1)S(1)}, bf16[2,2,16,512]{3,2,1,0:T(8,128)(2,1)S(1)}, u32[]{:S(2)}, u32[]{:S(2)}) collective-permute-start(bf16[2,2,16,512]{3,2,1,0:T(8,128)(2,1)S(1)} %get-tuple-element.58), channel_id=1, source_target_pairs={{0,32},{32,64},{64,96},{96,128},{128,160},{160,192},{192,224},{224... | collective-permute-start | bytes 196616 | tf_op jit(solution)/shard_map/ppermute | solution.py:20
  74.8 1.3 collective-permute-start.7
  76.7 3.8 %collective-permute-done.7 = bf16[2,2,16,512]{3,2,1,0:T(8,128)(2,1)S(1)} collective-permute-done((bf16[2,2,16,512]{3,2,1,0:T(8,128)(2,1)S(1)}, bf16[2,2,16,512]{3,2,1,0:T(8,128)(2,1)S(1)}, u32[]{:S(2)}, u32[]{:S(2)}) %collective-permute-start.7) | collective-permute-done | bytes 65568 | tf_op jit(solution)/shard_map/ppermute | solution.py:22
  81.3 6.1 %collective-permute-start.8 = (bf16[2,2,64,16]{3,2,1,0:T(8,128)(2,1)S(1)}, bf16[2,2,64,16]{3,2,1,0:T(8,128)(2,1)S(1)}, u32[]{:S(2)}, u32[]{:S(2)}) collective-permute-start(bf16[2,2,64,16]{3,2,1,0:T(8,128)(2,1)S(1)} %get-tuple-element.56), channel_id=1, source_target_pairs={{0,4},{4,8},{8,12},{12,16},{16,20},{20,24},{24,28},{1,5},{5,9},{9,... | collective-permute-start | bytes 24584 | tf_op jit(solution)/shard_map/ppermute | solution.py:20
  87.5 1.3 collective-permute-start.9
  90.7 3.0 %collective-permute-done.9 = bf16[2,2,64,16]{3,2,1,0:T(8,128)(2,1)S(1)} collective-permute-done((bf16[2,2,64,16]{3,2,1,0:T(8,128)(2,1)S(1)}, bf16[2,2,64,16]{3,2,1,0:T(8,128)(2,1)S(1)}, u32[]{:S(2)}, u32[]{:S(2)}) %collective-permute-start.9) | collective-permute-done | bytes 8224 | tf_op jit(solution)/shard_map/ppermute | solution.py:22
  95.8 4.6 %collective-permute-start.10 = (bf16[2,2,16,512]{3,2,1,0:T(8,128)(2,1)S(1)}, bf16[2,2,16,512]{3,2,1,0:T(8,128)(2,1)S(1)}, u32[]{:S(2)}, u32[]{:S(2)}) collective-permute-start(bf16[2,2,16,512]{3,2,1,0:T(8,128)(2,1)S(1)} %get-tuple-element.54), channel_id=1, source_target_pairs={{0,32},{32,64},{64,96},{96,128},{128,160},{160,192},{192,224},{224... | collective-permute-start | bytes 196616 | tf_op jit(solution)/shard_map/ppermute | solution.py:20
  100.4 1.3 collective-permute-start.11
  102.3 3.1 %collective-permute-done.11 = bf16[2,2,16,512]{3,2,1,0:T(8,128)(2,1)S(1)} collective-permute-done((bf16[2,2,16,512]{3,2,1,0:T(8,128)(2,1)S(1)}, bf16[2,2,16,512]{3,2,1,0:T(8,128)(2,1)S(1)}, u32[]{:S(2)}, u32[]{:S(2)}) %collective-permute-start.11) | collective-permute-done | bytes 65568 | tf_op jit(solution)/shard_map/ppermute | solution.py:22
  107.4 52.4 %reduce-scatter.2.cloned.1.call-done = bf16[16,512]{1,0:T(8,128)(2,1)} async-done(((bf16[64,512]{1,0:T(8,128)(2,1)}), bf16[16,512]{1,0:T(8,128)(2,1)}) %reduce-scatter.2.cloned.1.call-update) | async-done | bytes 16400 | tf_op jit(solution)/shard_map/reduce_scatter | solution.py:127
  159.9 1.3 convert_multiply_fusion
  (167 shorter events, 40.7 us)
Async XLA Ops:
  7.2 152.7 %reduce-scatter.2.cloned.1.call-start = ((), (), s32[]{:S(2)}) async-start(), calls=%async_computation.1 | async-start | bytes 81920 | tf_op jit(solution)/shard_map/reduce_scatter | solution.py:127
  8.8 36.3 %collective-permute-start = (bf16[2,2,64,16]{3,2,1,0:T(8,128)(2,1)}, bf16[2,2,64,16]{3,2,1,0:T(8,128)(2,1)}, u32[]{:S(2)}, u32[]{:S(2)}) collective-permute-start(bf16[2,2,64,16]{3,2,1,0:T(8,128)(2,1)} %get-tuple-element.64), channel_id=1, source_target_pairs={{0,4},{4,8},{8,12},{12,16},{16,20},{20,24},{24,28},{1,5},{5,9},{9,... | collective-permute-start | bytes 24584 | tf_op jit(solution)/shard_map/ppermute | solution.py:20
  15.1 30.0 %collective-permute-start.1 = (bf16[2,2,64,16]{3,2,1,0:T(8,128)(2,1)S(1)}, bf16[2,2,64,16]{3,2,1,0:T(8,128)(2,1)}, u32[]{:S(2)}, u32[]{:S(2)}) collective-permute-start(bf16[2,2,64,16]{3,2,1,0:T(8,128)(2,1)S(1)} %get-tuple-element.65), channel_id=1, source_target_pairs={{4,0},{8,4},{12,8},{16,12},{20,16},{24,20},{28,24},{5,1},{9,5},{13... | collective-permute-start | bytes 24584 | tf_op jit(solution)/shard_map/ppermute | solution.py:22
  20.5 1.0 copy-start.5
  26.8 0.7 copy-start.6
  27.1 14.6 %copy-start = (bf16[1,2,4,20480]{3,2,1,0:T(4,128)(2,1)S(1)}, bf16[1,2,4,20480]{3,2,1,0:T(4,128)(2,1)}, u32[]{:S(2)}) copy-start(bf16[1,2,4,20480]{3,2,1,0:T(4,128)(2,1)} %get-tuple-element.34) | copy-start | bytes 983044
  43.4 1.7 %copy-start.1 = (bf16[2,2,64,512]{3,2,1,0:T(8,128)(2,1)S(1)}, bf16[2,2,64,512]{3,2,1,0:T(8,128)(2,1)}, u32[]{:S(2)}) copy-start(bf16[2,2,64,512]{3,2,1,0:T(8,128)(2,1)} %param.8) | copy-start | bytes 786436
  47.1 1.0 copy-start.2
  48.8 5.2 %collective-permute-start.2 = (bf16[2,2,16,512]{3,2,1,0:T(8,128)(2,1)S(1)}, bf16[2,2,16,512]{3,2,1,0:T(8,128)(2,1)S(1)}, u32[]{:S(2)}, u32[]{:S(2)}) collective-permute-start(bf16[2,2,16,512]{3,2,1,0:T(8,128)(2,1)S(1)} %get-tuple-element.62), channel_id=1, source_target_pairs={{0,32},{32,64},{64,96},{96,128},{128,160},{160,192},{192,224},{224... | collective-permute-start | bytes 196616 | tf_op jit(solution)/shard_map/ppermute | solution.py:20
  51.9 5.0 %collective-permute-start.3 = (bf16[2,2,16,512]{3,2,1,0:T(8,128)(2,1)S(1)}, bf16[2,2,16,512]{3,2,1,0:T(8,128)(2,1)S(1)}, u32[]{:S(2)}, u32[]{:S(2)}) collective-permute-start(bf16[2,2,16,512]{3,2,1,0:T(8,128)(2,1)S(1)} %get-tuple-element.63), channel_id=1, source_target_pairs={{32,0},{64,32},{96,64},{128,96},{160,128},{192,160},{224,192},{256... | collective-permute-start | bytes 196616 | tf_op jit(solution)/shard_map/ppermute | solution.py:22
  56.9 0.8 copy-start.4
  58.1 8.4 %collective-permute-start.4 = (bf16[2,2,64,16]{3,2,1,0:T(8,128)(2,1)S(1)}, bf16[2,2,64,16]{3,2,1,0:T(8,128)(2,1)S(1)}, u32[]{:S(2)}, u32[]{:S(2)}) collective-permute-start(bf16[2,2,64,16]{3,2,1,0:T(8,128)(2,1)S(1)} %get-tuple-element.60), channel_id=1, source_target_pairs={{0,4},{4,8},{8,12},{12,16},{16,20},{20,24},{24,28},{1,5},{5,9},{9,... | collective-permute-start | bytes 24584 | tf_op jit(solution)/shard_map/ppermute | solution.py:20
  63.0 6.6 %collective-permute-start.5 = (bf16[2,2,64,16]{3,2,1,0:T(8,128)(2,1)S(1)}, bf16[2,2,64,16]{3,2,1,0:T(8,128)(2,1)S(1)}, u32[]{:S(2)}, u32[]{:S(2)}) collective-permute-start(bf16[2,2,64,16]{3,2,1,0:T(8,128)(2,1)S(1)} %get-tuple-element.61), channel_id=1, source_target_pairs={{4,0},{8,4},{12,8},{16,12},{20,16},{24,20},{28,24},{5,1},{9,5},{13... | collective-permute-start | bytes 24584 | tf_op jit(solution)/shard_map/ppermute | solution.py:22
  71.7 5.0 %collective-permute-start.6 = (bf16[2,2,16,512]{3,2,1,0:T(8,128)(2,1)S(1)}, bf16[2,2,16,512]{3,2,1,0:T(8,128)(2,1)S(1)}, u32[]{:S(2)}, u32[]{:S(2)}) collective-permute-start(bf16[2,2,16,512]{3,2,1,0:T(8,128)(2,1)S(1)} %get-tuple-element.58), channel_id=1, source_target_pairs={{0,32},{32,64},{64,96},{96,128},{128,160},{160,192},{192,224},{224... | collective-permute-start | bytes 196616 | tf_op jit(solution)/shard_map/ppermute | solution.py:20
  74.8 5.7 %collective-permute-start.7 = (bf16[2,2,16,512]{3,2,1,0:T(8,128)(2,1)S(1)}, bf16[2,2,16,512]{3,2,1,0:T(8,128)(2,1)S(1)}, u32[]{:S(2)}, u32[]{:S(2)}) collective-permute-start(bf16[2,2,16,512]{3,2,1,0:T(8,128)(2,1)S(1)} %get-tuple-element.59), channel_id=1, source_target_pairs={{32,0},{64,32},{96,64},{128,96},{160,128},{192,160},{224,192},{256... | collective-permute-start | bytes 196616 | tf_op jit(solution)/shard_map/ppermute | solution.py:22
  81.3 9.3 %collective-permute-start.8 = (bf16[2,2,64,16]{3,2,1,0:T(8,128)(2,1)S(1)}, bf16[2,2,64,16]{3,2,1,0:T(8,128)(2,1)S(1)}, u32[]{:S(2)}, u32[]{:S(2)}) collective-permute-start(bf16[2,2,64,16]{3,2,1,0:T(8,128)(2,1)S(1)} %get-tuple-element.56), channel_id=1, source_target_pairs={{0,4},{4,8},{8,12},{12,16},{16,20},{20,24},{24,28},{1,5},{5,9},{9,... | collective-permute-start | bytes 24584 | tf_op jit(solution)/shard_map/ppermute | solution.py:20
  87.5 6.2 %collective-permute-start.9 = (bf16[2,2,64,16]{3,2,1,0:T(8,128)(2,1)S(1)}, bf16[2,2,64,16]{3,2,1,0:T(8,128)(2,1)S(1)}, u32[]{:S(2)}, u32[]{:S(2)}) collective-permute-start(bf16[2,2,64,16]{3,2,1,0:T(8,128)(2,1)S(1)} %get-tuple-element.57), channel_id=1, source_target_pairs={{4,0},{8,4},{12,8},{16,12},{20,16},{24,20},{28,24},{5,1},{9,5},{13... | collective-permute-start | bytes 24584 | tf_op jit(solution)/shard_map/ppermute | solution.py:22
  95.6 6.1 %copy-start.3 = (f32[8,3,8,512]{3,1,2,0:T(4,128)S(1)}, f32[8,3,8,512]{3,1,2,0:T(4,128)}, u32[]{:S(2)}) copy-start(f32[8,3,8,512]{3,1,2,0:T(4,128)} %get-tuple-element.24) | copy-start | bytes 1179652
  95.8 6.5 %collective-permute-start.10 = (bf16[2,2,16,512]{3,2,1,0:T(8,128)(2,1)S(1)}, bf16[2,2,16,512]{3,2,1,0:T(8,128)(2,1)S(1)}, u32[]{:S(2)}, u32[]{:S(2)}) collective-permute-start(bf16[2,2,16,512]{3,2,1,0:T(8,128)(2,1)S(1)} %get-tuple-element.54), channel_id=1, source_target_pairs={{0,32},{32,64},{64,96},{96,128},{128,160},{160,192},{192,224},{224... | collective-permute-start | bytes 196616 | tf_op jit(solution)/shard_map/ppermute | solution.py:20
  100.4 5.0 %collective-permute-start.11 = (bf16[2,2,16,512]{3,2,1,0:T(8,128)(2,1)S(1)}, bf16[2,2,16,512]{3,2,1,0:T(8,128)(2,1)S(1)}, u32[]{:S(2)}, u32[]{:S(2)}) collective-permute-start(bf16[2,2,16,512]{3,2,1,0:T(8,128)(2,1)S(1)} %get-tuple-element.55), channel_id=1, source_target_pairs={{32,0},{64,32},{96,64},{128,96},{160,128},{192,160},{224,192},{256... | collective-permute-start | bytes 196616 | tf_op jit(solution)/shard_map/ppermute | solution.py:22
Sparse Core Ops, SparseCore 0:
  106.6 53.2 reduce-scatter.1
where the time goes:
time: 169 us; the launch traced here: 168 us
  waiting for transfers between devices  68.5 us (41%)
  starting transfers between devices  36.2 us (21%)
  local copies, waits for them, and re-layouts  28.4 us (17%)
  between operations  15 us (9%)
  matrix products  13.1 us (8%)
  other arithmetic  6.91 us (4%)
    reduce_scatter x1, waiting for transfers between devices, shards(): lax.psum_scatter(image_part.astype(jnp.bfloat16), 'freq', scatter_dimensi...  52.4 us
    ppermute x6, starting transfers between devices, padded_2(): lax.ppermute(tail, axis, [(i, (i + 1) % count) for i in range(ends)])  28.2 us
    ppermute x6, waiting for transfers between devices, padded_2(): lax.ppermute(head, axis, [((i + 1) % count, i) for i in range(ends)])  16 us
    dot_general x8, matrix products, one_block(): jnp.einsum('srh,zh->zsr', onehot, bin_weight, precision=lax.Precision.HIG...  8.4 us
    ppermute x6, starting transfers between devices, padded_2(): lax.ppermute(head, axis, [((i + 1) % count, i) for i in range(ends)])  7.92 us
    squeeze x18, local copies, waits for them, and re-layouts, operator_pair(): real_part = jnp.concatenate([matrices[0], -matrices[1]], axis=-1)  5.86 us
    eq x8, local copies, waits for them, and re-layouts, one_block(): bins_block[:, :, None] == jnp.arange(bin_count, dtype=jnp.int32)  5.75 us
    reshape x6, local copies, waits for them, and re-layouts, banded(): padded.reshape(leading + (block_count, block_size * (tap_count + block_si...  5.41 us
  transfers between devices with their start and end apart: 13, of which 6 were waited for; matrix products, arithmetic and copies ran while one was open for 21% of the time, Pallas kernels for 0%

commit v1 on v0

v1 whole, which is shorter than its diff:
```python
import functools
import math

import jax
import jax.numpy as jnp
from jax import lax
from jax.experimental import pallas as pl
from jax.experimental.pallas import tpu as pltpu
from jax.sharding import PartitionSpec as P

MESH = pl.DeviceIdType.MESH
TAPS = 33
HALF = TAPS // 2
DEPTHS = 3
HALO = HALF * DEPTHS
LANE = 128
PAD = LANE
BF = jnp.bfloat16
F32 = jnp.float32


def across(a, b):
    return lax.dot_general(a, b, (((1,), (1,)), ((), ())), preferred_element_type=F32)


def columns_of(rows):
    n = rows.shape[1]
    eye = lax.broadcasted_iota(jnp.int32, (n, n), 0) == lax.broadcasted_iota(jnp.int32, (n, n), 1)
    return across(eye.astype(BF), rows.astype(F32).astype(BF))


def onehot_of(column, entries):
    places = lax.broadcasted_iota(jnp.int32, (column.shape[0], entries), 1).astype(F32)
    return jnp.where(column == places, 1.0, 0.0).astype(BF)


def band(taps, base):
    m = taps.shape[0]
    turned = pltpu.roll(taps, base, 1, stride=1, stride_axis=0)
    lane = lax.broadcasted_iota(jnp.int32, (m, LANE), 1)
    row = lax.broadcasted_iota(jnp.int32, (m, LANE), 0)
    place = lane - row - base
    first = jnp.where(place >= 0, turned, 0.0)
    second = jnp.where((place < 0) & (place >= -LANE), turned, 0.0)
    return first.astype(BF), second.astype(BF)


def kernel(
    sizes,
    wave,
    table,
    src_index,
    rec_index,
    offset_bin,
    bin_weight,
    wave_out,
    image_out,
    x0,
    x1,
    x2,
    q,
    fin,
    src_low,
    src_high,
    rec_low,
    rec_high,
    src_col,
    rec_col,
    taps_table,
    rec_taps,
    rec_op,
    src_op0,
    src_op1,
    src_op2,
    weights,
    part,
    part_bf,
    parts_in,
    own_sem,
    out_sem,
    send_sem,
    recv_sem,
    index_send,
    index_recv,
    part_send,
    part_recv,
):
    n_src, n_rec, n_freq, scale = sizes
    _, n_f, rows, cols = wave.shape
    entries = table.shape[1]
    tiles = cols // LANE
    i, j, g = lax.axis_index("src"), lax.axis_index("rec"), lax.axis_index("freq")
    has = {-1: (i > 0, j > 0), 0: (None, None), 1: (i < n_src - 1, j < n_rec - 1)}
    ways = [(0, -1), (0, 1), (-1, 0), (1, 0), (-1, -1), (-1, 1), (1, -1), (1, 1)]

    def exists(way):
        conds = [c for c in (has[way[0]][0], has[way[1]][1]) if c is not None]
        return functools.reduce(jnp.logical_and, conds)

    def target(way):
        where = {}
        if way[0]:
            where["src"] = i + way[0]
        if way[1]:
            where["rec"] = j + way[1]
        return where

    for f in range(n_f):
        for c in range(2):
            x0[f, c, :HALO, :] = jnp.zeros((HALO, cols + 2 * PAD), BF)
            x0[f, c, HALO + rows :, :] = jnp.zeros((HALO, cols + 2 * PAD), BF)
            x0[f, c, HALO : HALO + rows, :PAD] = jnp.zeros((rows, PAD), BF)
            x0[f, c, HALO : HALO + rows, PAD + cols :] = jnp.zeros((rows, PAD), BF)
    for ref in (src_low, src_high, rec_low, rec_high):
        ref[...] = jnp.full(ref.shape, -1, jnp.int32)

    barrier = pltpu.get_barrier_semaphore()
    for way in ways:

        @pl.when(exists(way))
        def _(way=way):
            pl.semaphore_signal(barrier, inc=1, device_id=target(way), device_id_type=MESH)

    for d in range(1, n_freq):
        pl.semaphore_signal(
            barrier, inc=1, device_id={"freq": lax.rem(g + d, n_freq)}, device_id_type=MESH
        )
    along_src = (i > 0).astype(jnp.int32) + (i < n_src - 1).astype(jnp.int32)
    along_rec = (j > 0).astype(jnp.int32) + (j < n_rec - 1).astype(jnp.int32)

    own = [
        pltpu.make_async_copy(
            wave.at[:, f],
            x0.at[f, :, pl.ds(HALO, rows), pl.ds(PAD, cols)],
            own_sem.at[f],
        )
        for f in range(n_f)
    ]
    for copy in own:
        copy.start()
    pl.semaphore_wait(barrier, (along_src + 1) * (along_rec + 1) - 1 + n_freq - 1)

    def halo_copy(f, number, way):
        ds, dr = way
        if ds == 0:
            from_rows, to_rows = pl.ds(0, rows), pl.ds(HALO, rows)
        elif ds < 0:
            from_rows, to_rows = pl.ds(0, HALO), pl.ds(HALO + rows, HALO)
        else:
            from_rows, to_rows = pl.ds(rows - HALO, HALO), pl.ds(0, HALO)
        if dr == 0:
            from_cols, to_cols = pl.ds(0, cols), pl.ds(PAD, cols)
        elif dr < 0:
            from_cols, to_cols = pl.ds(0, PAD), pl.ds(PAD + cols, PAD)
        else:
            from_cols, to_cols = pl.ds(cols - PAD, PAD), pl.ds(0, PAD)
        return pltpu.make_async_remote_copy(
            src_ref=wave.at[:, f, from_rows, from_cols],
            dst_ref=x0.at[f, :, to_rows, to_cols],
            send_sem=send_sem.at[f, number],
            recv_sem=recv_sem.at[f, number],
            device_id=target(way),
            device_id_type=MESH,
        )

    def index_copy(number, way):
        if way[0]:
            source, dest = src_index, (src_high if way[0] < 0 else src_low)
        elif way[1] < 0:
            source, dest = rec_index.at[:, pl.ds(0, PAD)], rec_high
        else:
            source, dest = rec_index.at[:, pl.ds(cols - PAD, PAD)], rec_low
        return pltpu.make_async_remote_copy(
            src_ref=source,
            dst_ref=dest,
            send_sem=index_send.at[number],
            recv_sem=index_recv.at[number],
            device_id=target(way),
            device_id_type=MESH,
        )

    for number, way in enumerate(ways[:4]):

        @pl.when(exists(way))
        def _(number=number, way=way):
            index_copy(number, way).start()

    for f in range(n_f):
        for number, way in enumerate(ways):

            @pl.when(exists(way))
            def _(f=f, number=number, way=way):
                halo_copy(f, number, way).start()

    taps_table[...] = jnp.zeros(taps_table.shape, BF)
    for f in range(n_f):
        for c in range(2):
            first = (2 * f + c) * LANE
            taps_table[:, first : first + TAPS] = table[c, :, f, :].astype(BF)

    for t in range(tiles):
        at = slice(t * LANE, (t + 1) * LANE)
        bins = offset_bin[:, at]
        for z in range(DEPTHS):
            line = jnp.concatenate(
                [bin_weight[z : z + 1, :], jnp.zeros((1, LANE - bin_weight.shape[1]), F32)], axis=1
            )
            spread = jnp.broadcast_to(line, (rows, LANE))
            weights[z, :, at] = jnp.take_along_axis(
                spread, bins, axis=1, mode="promise_in_bounds"
            )

    for number, way in enumerate(ways[:4]):

        @pl.when(exists(way))
        def _(number=number, way=way):
            index_copy(number, way).wait_send()

        @pl.when(exists((-way[0], -way[1])))
        def _(number=number, way=way):
            index_copy(number, way).wait_recv()

    src_col[:rows, :] = columns_of(src_low[...])
    src_col[rows : 2 * rows, :] = columns_of(src_index[...])
    src_col[2 * rows :, :] = columns_of(src_high[...])
    rec_col[:PAD, :] = columns_of(rec_low[...])
    for t in range(tiles):
        rec_col[PAD + t * LANE : PAD + (t + 1) * LANE, :] = columns_of(
            rec_index[:, t * LANE : (t + 1) * LANE]
        )
    rec_col[PAD + cols :, :] = columns_of(rec_high[...])

    for z, op in enumerate((src_op0, src_op1, src_op2)):
        left = HALO - HALF * (z + 1)
        n_out = rows + 2 * left
        hot = onehot_of(src_col[rows - left : rows - left + n_out, z : z + 1], entries)
        taps = jnp.dot(hot, taps_table[...], preferred_element_type=F32)
        for f in range(n_f):
            for c in range(2):
                first, second = band(taps[:, (2 * f + c) * LANE : (2 * f + c + 1) * LANE], 0)
                op[f, c * n_out : (c + 1) * n_out, :LANE] = first
                if op.shape[2] > LANE:
                    op[f, c * n_out : (c + 1) * n_out, LANE:] = second

    counts = [tiles + 1, tiles + 1, tiles]
    starts = [0, counts[0], counts[0] + counts[1]]
    for z in range(DEPTHS):
        left = HALO - HALF * (z + 1)
        base = PAD - left - HALF if z == 0 else 0

        def build(n, carry, z=z, left=left, base=base):
            at = pl.multiple_of(n * LANE + (PAD - left), HALF)
            hot = onehot_of(rec_col[pl.ds(at, LANE), :][:, z : z + 1], entries)
            rec_taps[...] = jnp.dot(hot, taps_table[...], preferred_element_type=F32)
            for f in range(n_f):
                for c in range(2):
                    first, second = band(rec_taps[:, (2 * f + c) * LANE : (2 * f + c + 1) * LANE], base)
                    rec_op[f, starts[z] + n, c * LANE : (c + 1) * LANE, :LANE] = first
                    rec_op[f, starts[z] + n, c * LANE : (c + 1) * LANE, LANE:] = second
            return carry

        lax.fori_loop(0, counts[z], build, 0)

    for f in range(n_f):
        own[f].wait()
        for number, way in enumerate(ways):

            @pl.when(exists((-way[0], -way[1])))
            def _(f=f, number=number, way=way):
                halo_copy(f, number, way).wait_recv()

        held = (x0.at[f], x1, x2)
        for z in range(DEPTHS):
            left = HALO - HALF * (z + 1)
            n_in, n_out = rows + 2 * left + 2 * HALF, rows + 2 * left
            source = held[z]
            for n in range(counts[z]):
                wide = 2 * LANE if (n + 2) * LANE <= source.shape[-1] else LANE
                window = source[:, :, n * LANE : n * LANE + wide].reshape(2 * n_in, wide)
                y = across(window, rec_op[f, starts[z] + n, :, :wide])
                at = slice(n * LANE, (n + 1) * LANE)
                q[0, :n_in, at] = (y[:n_in, :LANE] - y[n_in:, LANE:]).astype(BF)
                q[1, :n_in, at] = (y[:n_in, LANE:] + y[n_in:, :LANE]).astype(BF)
            op = (src_op0, src_op1, src_op2)[z][f, :, :n_in]
            reals = []
            for n in range(counts[z]):
                at = slice(n * LANE, (n + 1) * LANE)
                pair = jnp.concatenate([q[0, :n_in, at], q[1, :n_in, at]], axis=1)
                y = jnp.dot(op, pair, preferred_element_type=F32)
                real = (y[:n_out, :LANE] - y[n_out:, LANE:]).astype(BF)
                imag = (y[:n_out, LANE:] + y[n_out:, :LANE]).astype(BF)
                if z + 1 < DEPTHS:
                    held[z + 1][0, :, at] = real
                    held[z + 1][1, :, at] = imag
                else:
                    fin[0, f, :, at] = real
                    fin[1, f, :, at] = imag
                reals.append(real[left : left + rows, :].astype(F32))
            whole = jnp.concatenate(reals, axis=1) if left else None
            if left:
                whole = pltpu.roll(whole, whole.shape[1] - left, 1)
            for t in range(tiles):
                at = slice(t * LANE, (t + 1) * LANE)
                term = weights[z, :, at] * (whole[:, at] if left else reals[t])
                if z == 0 and f == 0:
                    part[:, at] = term
                else:
                    part[:, at] = part[:, at] + term
        if f == n_f - 1:
            part_bf[...] = part[...].astype(BF)
            piece = rows // n_freq
            sends = []
            for d in range(1, n_freq):
                to = lax.rem(g + d, n_freq)
                copy = pltpu.make_async_remote_copy(
                    src_ref=part_bf.at[pl.ds(pl.multiple_of(to * piece, piece), piece)],
                    dst_ref=parts_in.at[d - 1],
                    send_sem=part_send.at[d - 1],
                    recv_sem=part_recv.at[d - 1],
                    device_id={"freq": to},
                    device_id_type=MESH,
                )
                copy.start()
                sends.append(copy)
        pltpu.make_async_copy(fin.at[:, f], wave_out.at[:, f], out_sem.at[f]).start()

    piece = rows // n_freq
    total = part_bf[pl.ds(pl.multiple_of(g * piece, piece), piece), :].astype(F32)
    for d, copy in enumerate(sends):
        copy.wait()
        total = total + parts_in[d].astype(F32)
    image_out[...] = total * scale

    for f in range(n_f):
        pltpu.make_async_copy(fin.at[:, f], wave_out.at[:, f], out_sem.at[f]).wait()
        for number, way in enumerate(ways):

            @pl.when(exists(way))
            def _(f=f, number=number, way=way):
                halo_copy(f, number, way).wait_send()


def shards(wave, tap_table, src_index, rec_index, offset_bin, bin_weight):
    n_src, n_rec, n_freq = (lax.axis_size(a) for a in ("src", "rec", "freq"))
    _, n_f, rows, cols = wave.shape
    scale = 1.0 / math.sqrt(n_f * n_freq * DEPTHS)
    tiles = cols // LANE
    piece = rows // n_freq
    outs = [rows + 2 * (HALO - HALF * (z + 1)) for z in range(DEPTHS)]
    vmem = pl.BlockSpec(memory_space=pltpu.VMEM)
    anywhere = pl.BlockSpec(memory_space=pl.ANY)
    dma = pltpu.SemaphoreType.DMA
    return pl.pallas_call(
        functools.partial(kernel, (n_src, n_rec, n_freq, scale)),
        out_shape=(
            jax.ShapeDtypeStruct(wave.shape, BF),
            jax.ShapeDtypeStruct((piece, cols), F32),
        ),
        in_specs=[anywhere, vmem, vmem, vmem, vmem, vmem],
        out_specs=(anywhere, vmem),
        scratch_shapes=[
            pltpu.VMEM((n_f, 2, rows + 2 * HALO, cols + 2 * PAD), BF),
            pltpu.VMEM((2, outs[0], cols + LANE), BF),
            pltpu.VMEM((2, outs[1], cols + LANE), BF),
            pltpu.VMEM((2, rows + 2 * HALO, cols + LANE), BF),
            pltpu.VMEM((2, n_f, rows, cols), BF),
            pltpu.VMEM((DEPTHS, rows), jnp.int32),
            pltpu.VMEM((DEPTHS, rows), jnp.int32),
            pltpu.VMEM((DEPTHS, PAD), jnp.int32),
            pltpu.VMEM((DEPTHS, PAD), jnp.int32),
            pltpu.VMEM((3 * rows, DEPTHS), F32),
            pltpu.VMEM((cols + 2 * PAD, DEPTHS), F32),
            pltpu.VMEM((tap_table.shape[1], n_f * 2 * LANE), BF),
            pltpu.VMEM((LANE, n_f * 2 * LANE), F32),
            pltpu.VMEM((n_f, 3 * tiles + 2, 2 * LANE, 2 * LANE), BF),
            pltpu.VMEM((n_f, 2 * outs[0], 2 * LANE), BF),
            pltpu.VMEM((n_f, 2 * outs[1], LANE), BF),
            pltpu.VMEM((n_f, 2 * outs[2], LANE), BF),
            pltpu.VMEM((DEPTHS, rows, cols), F32),
            pltpu.VMEM((rows, cols), F32),
            pltpu.VMEM((rows, cols), BF),
            pltpu.VMEM((max(n_freq - 1, 1), piece, cols), BF),
            dma((n_f,)),
            dma((n_f,)),
            dma((n_f, 8)),
            dma((n_f, 8)),
            dma((4,)),
            dma((4,)),
            dma((max(n_freq - 1, 1),)),
            dma((max(n_freq - 1, 1),)),
        ],
        compiler_params=pltpu.CompilerParams(
            collective_id=0, has_side_effects=True, vmem_limit_bytes=32 * 1024 * 1024
        ),
    )(wave, tap_table, src_index, rec_index, offset_bin, bin_weight)


def solution(mesh):
    placed = (
        P(None, "freq", "src", "rec"),
        P(None, None, "freq", None),
        P(None, "src"),
        P(None, "rec"),
        P("src", "rec"),
        P(),
    )
    return jax.shard_map(
        shards,
        mesh=mesh,
        in_specs=placed,
        out_specs=(P(None, "freq", "src", "rec"), P(("src", "freq"), "rec")),
        check_vma=False,
    )
```

time: 169 us -> 36.4 us (0.22)
  waiting for transfers between devices: 68.5 us -> 0 us
  starting transfers between devices: 36.2 us -> 0 us
  Pallas kernels: 0 us -> 32.1 us
  local copies, waits for them, and re-layouts: 28.4 us -> 3.35 us
  between operations: 15 us -> 0.71 us
  matrix products: 13.1 us -> 0 us
  other arithmetic: 6.91 us -> 0 us
    reduce_scatter x1 -> x0, waiting for transfers between devices: 52.4 us -> none  [shards(): lax.psum_scatter(image_part.astype(jnp.bfloat16), 'freq', scatter_dimensi...]
    ppermute x12 -> x0, starting transfers between devices: 36.1 us -> none  [the longest x6 28.2 us: padded_2(): lax.ppermute(tail, axis, [(i, (i + 1) % count) for i in range(ends)])]
    pallas_call x0 -> x1, Pallas kernels: none -> 32.1 us  [shards(): pl.pallas_call(functools.partial(kernel, (n_src, n_rec, n_freq, scale)),...]
    ppermute x12 -> x0, waiting for transfers between devices: 16 us -> none  [the longest x6 16 us: padded_2(): lax.ppermute(head, axis, [((i + 1) % count, i) for i in range(ends)])]
    dot_general x26 -> x0, matrix products: 13.1 us -> none  [the longest x8 8.4 us: one_block(): jnp.einsum('srh,zh->zsr', onehot, bin_weight, precision=lax.Precision.HIG...]
    reshape x9 -> x0, local copies, waits for them, and re-layouts: 6.53 us -> none  [the longest x6 5.41 us: banded(): padded.reshape(leading + (block_count, block_size * (tap_count + block_si...]
    squeeze x21 -> x0, local copies, waits for them, and re-layouts: 5.97 us -> none  [the longest x18 5.86 us: operator_pair(): real_part = jnp.concatenate([matrices[0], -matrices[1]], axis=-1)]
    eq x9 -> x0, local copies, waits for them, and re-layouts: 5.75 us -> none  [the longest x8 5.75 us: one_block(): bins_block[:, :, None] == jnp.arange(bin_count, dtype=jnp.int32)]
  transfers between devices with their start and end apart: 13 -> 0, of which waited for: 6 -> 0; matrix products, arithmetic and copies ran while one was open for 21% -> 0% of each run, Pallas kernels for 0% -> 0%
where the time goes in v1:
time: 36.4 us; the launch traced here: 36.2 us
  Pallas kernels  32.1 us (88%)
  local copies, waits for them, and re-layouts  3.35 us (9%)
  between operations  0.71 us (2%)
    pallas_call x1, Pallas kernels, shards(): pl.pallas_call(functools.partial(kernel, (n_src, n_rec, n_freq, scale)),...  32.1 us
    unnamed x13, local copies, waits for them, and re-layouts  3.35 us

profile of v1, /device:TPU:1, one launch (start us, length us, event | category | flops | bytes accessed | tf_op | source)
XLA Modules:
  0.0 36.2 jit_solution(7678468468341494948)
XLA Ops:
  0.6 0.0 copy-start.4
  0.6 0.0 copy-start.1
  0.7 0.0 copy-start.2
  0.7 0.0 copy-start.3
  0.7 1.1 %copy.8.table = f32[2,64,2,33]{3,2,1,0:T(2,128)S(1)} copy(f32[2,64,2,33]{1,2,3,0:T(2,128)} %param.7) | data formatting | bytes 67584 | tf_op args[1]
  1.7 0.0 copy-done.4
  1.8 0.0 copy-done.1
  1.8 0.0 copy-done.2
  1.8 0.0 copy-done.3
  1.8 0.0 copy-start
  1.8 0.9 %copy-done = bf16[2,2,64,512]{3,2,1,0:T(8,128)(2,1)S(1)} copy-done((bf16[2,2,64,512]{3,2,1,0:T(8,128)(2,1)S(1)}, bf16[2,2,64,512]{3,2,1,0:T(8,128)(2,1)}, u32[]{:S(2)}) %copy-start) | copy-done | bytes 262168
  2.7 32.1 %shard_map.77 = (bf16[2,2,64,512]{3,2,1,0:T(8,128)(2,1)S(1)}, f32[16,512]{1,0:T(8,128)S(1)}) custom-call(bf16[2,2,64,512]{3,2,1,0:T(8,128)(2,1)S(1)} %copy-done, f32[2,64,2,33]{3,2,1,0:T(2,128)S(1)} %copy.8.table, s32[3,64]{1,0:T(4,128)S(1)} %copy-done.3, s32[3,512]{1,0:T(4,128)S(1)} %copy-done.2, s32[64,512]{1,0:T(8,128)S(1)} %copy-done.1, ...), custom_call_target="tpu_custom_call" | custom-call | tf_op jit(solution)/shard_map/pallas_call | solution.py:353
  34.9 0.7 %copy.11 = bf16[2,2,64,512]{3,2,1,0:T(8,128)(2,1)} copy(bf16[2,2,64,512]{3,2,1,0:T(8,128)(2,1)S(1)} %get-tuple-element.4) | data formatting | bytes 524288
  35.6 0.6 %copy.12 = f32[16,512]{1,0:T(8,128)} copy(f32[16,512]{1,0:T(8,128)S(1)} %get-tuple-element.5) | data formatting | bytes 65536
Async XLA Ops:
  0.6 1.1 %copy-start.4 = (f32[3,64]{1,0:T(4,128)S(1)}, f32[3,64]{1,0:T(4,128)}, u32[]{:S(2)}) copy-start(f32[3,64]{1,0:T(4,128)} %bin_weight.1) | copy-start | bytes 2308
  0.6 1.1 %copy-start.1 = (s32[64,512]{1,0:T(8,128)S(1)}, s32[64,512]{1,0:T(8,128)}, u32[]{:S(2)}) copy-start(s32[64,512]{1,0:T(8,128)} %offset_bin.1) | copy-start | bytes 393220
  0.7 1.1 %copy-start.2 = (s32[3,512]{1,0:T(4,128)S(1)}, s32[3,512]{1,0:T(4,128)}, u32[]{:S(2)}) copy-start(s32[3,512]{1,0:T(4,128)} %rec_index.1) | copy-start | bytes 18436
  0.7 1.1 %copy-start.3 = (s32[3,64]{1,0:T(4,128)S(1)}, s32[3,64]{1,0:T(4,128)}, u32[]{:S(2)}) copy-start(s32[3,64]{1,0:T(4,128)} %src_index.1) | copy-start | bytes 2308
  1.8 1.0 %copy-start = (bf16[2,2,64,512]{3,2,1,0:T(8,128)(2,1)S(1)}, bf16[2,2,64,512]{3,2,1,0:T(8,128)(2,1)}, u32[]{:S(2)}) copy-start(bf16[2,2,64,512]{3,2,1,0:T(8,128)(2,1)} %wave.1) | copy-start | bytes 786436

commit v2 on v1

v2 whole, which is shorter than its diff:
```python
import functools
import math

import jax
import jax.numpy as jnp
from jax import lax
from jax.experimental import pallas as pl
from jax.experimental.pallas import tpu as pltpu
from jax.sharding import PartitionSpec as P

MESH = pl.DeviceIdType.MESH
TAPS = 33
HALF = TAPS // 2
DEPTHS = 3
HALO = HALF * DEPTHS
LANE = 128
PAD = LANE
BF = jnp.bfloat16
F32 = jnp.float32


def across(a, b):
    return lax.dot_general(a, b, (((1,), (1,)), ((), ())), preferred_element_type=F32)


def columns_of(rows):
    n = rows.shape[1]
    eye = lax.broadcasted_iota(jnp.int32, (n, n), 0) == lax.broadcasted_iota(jnp.int32, (n, n), 1)
    return across(eye.astype(BF), rows.astype(F32).astype(BF))


def onehot_of(column, entries):
    places = lax.broadcasted_iota(jnp.int32, (column.shape[0], entries), 1).astype(F32)
    return jnp.where(column == places, 1.0, 0.0).astype(BF)


def band(taps, base):
    m = taps.shape[0]
    turned = pltpu.roll(taps, base, 1, stride=1, stride_axis=0)
    lane = lax.broadcasted_iota(jnp.int32, (m, LANE), 1)
    row = lax.broadcasted_iota(jnp.int32, (m, LANE), 0)
    place = lane - row - base
    first = jnp.where(place >= 0, turned, 0.0)
    second = jnp.where((place < 0) & (place >= -LANE), turned, 0.0)
    return first.astype(BF), second.astype(BF)


def kernel(
    sizes,
    wave,
    table_in,
    src_index_in,
    rec_index_in,
    offset_bin_in,
    bin_weight_in,
    fin,
    part_own,
    parts_in,
    table,
    src_index,
    rec_index,
    offset_bin,
    bin_weight,
    in_sem,
    x0,
    x1,
    x2,
    q,
    src_low,
    src_high,
    rec_low,
    rec_high,
    src_col,
    rec_col,
    taps_table,
    rec_taps,
    rec_op,
    src_op0,
    src_op1,
    src_op2,
    weights,
    part,
    part_bf,
    own_sem,
    send_sem,
    recv_sem,
    index_send,
    index_recv,
    part_send,
    part_recv,
    ready,
    peer_ready,
):
    n_src, n_rec, n_freq = sizes
    _, n_f, rows, cols = wave.shape
    entries = table.shape[3]
    tiles = cols // LANE
    i, j, g = lax.axis_index("src"), lax.axis_index("rec"), lax.axis_index("freq")
    has = {-1: (i > 0, j > 0), 0: (None, None), 1: (i < n_src - 1, j < n_rec - 1)}
    ways = [(-1, 0), (1, 0), (0, -1), (0, 1), (-1, -1), (-1, 1), (1, -1), (1, 1)]

    def exists(way):
        conds = [c for c in (has[way[0]][0], has[way[1]][1]) if c is not None]
        return functools.reduce(jnp.logical_and, conds)

    def target(way):
        where = {}
        if way[0]:
            where["src"] = i + way[0]
        if way[1]:
            where["rec"] = j + way[1]
        return where

    barrier = pltpu.get_barrier_semaphore()
    for way in ways:
        if way[1] >= 0:

            @pl.when(exists(way))
            def _(way=way):
                pl.semaphore_signal(barrier, inc=1, device_id=target(way), device_id_type=MESH)

    for d in range(1, n_freq):

        @pl.when(g >= d)
        def _(d=d):
            pl.semaphore_signal(barrier, inc=1, device_id={"freq": g - d}, device_id_type=MESH)

    fetch = [
        pltpu.make_async_copy(source, dest, in_sem.at[k])
        for k, (source, dest) in enumerate(
            [
                (src_index_in, src_index),
                (rec_index_in, rec_index),
                (table_in, table),
                (bin_weight_in, bin_weight),
                (offset_bin_in, offset_bin),
            ]
        )
    ]
    for copy in fetch:
        copy.start()
    own = [
        pltpu.make_async_copy(
            wave.at[:, f],
            x0.at[f, :, pl.ds(HALO, rows), pl.ds(PAD, cols)],
            own_sem.at[f],
        )
        for f in range(n_f)
    ]
    for copy in own:
        copy.start()

    along_src = (i > 0).astype(jnp.int32) + (i < n_src - 1).astype(jnp.int32)
    below_rec = (j > 0).astype(jnp.int32)

    def halo_copy(f, number, way):
        ds, dr = way
        from_rows = [pl.ds(0, rows), pl.ds(rows - HALO, HALO), pl.ds(0, HALO)][ds]
        to_rows = [pl.ds(HALO, rows), pl.ds(0, HALO), pl.ds(HALO + rows, HALO)][ds]
        from_cols = [pl.ds(0, cols), pl.ds(cols - PAD, PAD), pl.ds(0, PAD)][dr]
        to_cols = [pl.ds(PAD, cols), pl.ds(0, PAD), pl.ds(PAD + cols, PAD)][dr]
        return pltpu.make_async_remote_copy(
            src_ref=wave.at[:, f, from_rows, from_cols],
            dst_ref=x0.at[f, :, to_rows, to_cols],
            send_sem=send_sem.at[f, number],
            recv_sem=recv_sem.at[f, number],
            device_id=target(way),
            device_id_type=MESH,
        )

    def index_copy(number, way):
        if way[0]:
            source, dest = src_index_in, (src_high if way[0] < 0 else src_low)
        elif way[1] < 0:
            source, dest = rec_index_in.at[:, pl.ds(0, PAD)], rec_high
        else:
            source, dest = rec_index_in.at[:, pl.ds(cols - PAD, PAD)], rec_low
        return pltpu.make_async_remote_copy(
            src_ref=source,
            dst_ref=dest,
            send_sem=index_send.at[number],
            recv_sem=index_recv.at[number],
            device_id=target(way),
            device_id_type=MESH,
        )

    counts = [tiles + 1, tiles + 1, tiles]
    starts = [0, counts[0], counts[0] + counts[1]]
    lefts = [HALO - HALF * (z + 1) for z in range(DEPTHS)]

    def build_rec(z, blocks):
        base = PAD - lefts[z] - HALF if z == 0 else 0
        for n in blocks:
            at = n * LANE + PAD - lefts[z]
            hot = onehot_of(rec_col[at : at + LANE, z : z + 1], entries)
            slot = starts[z] + n
            rec_taps[slot] = across(hot, taps_table[...])
        for n in blocks:
            slot = starts[z] + n
            for f in range(n_f):
                for c in range(2):
                    first = (2 * f + c) * LANE
                    low, high = band(rec_taps[slot, :, first : first + LANE], base)
                    rec_op[f, slot, c * LANE : (c + 1) * LANE, :LANE] = low
                    rec_op[f, slot, c * LANE : (c + 1) * LANE, LANE:] = high

    def build_src(z):
        op = (src_op0, src_op1, src_op2)[z]
        n_out = rows + 2 * lefts[z]
        hot = onehot_of(src_col[rows - lefts[z] : rows - lefts[z] + n_out, z : z + 1], entries)
        taps = across(hot, taps_table[...])
        for f in range(n_f):
            for c in range(2):
                low, high = band(taps[:, (2 * f + c) * LANE : (2 * f + c + 1) * LANE], 0)
                op[f, c * n_out : (c + 1) * n_out, :LANE] = low
                if op.shape[2] > LANE:
                    op[f, c * n_out : (c + 1) * n_out, LANE:] = high

    for way in ways:

        @pl.when(jnp.logical_not(exists(way)))
        def _(way=way):
            ds, dr = way
            at_rows = [slice(HALO, HALO + rows), slice(HALO + rows, None), slice(0, HALO)][ds]
            at_cols = [slice(PAD, PAD + cols), slice(PAD + cols, None), slice(0, PAD)][dr]
            for f in range(n_f):
                for c in range(2):
                    shape = x0[f, c, at_rows, at_cols].shape
                    x0[f, c, at_rows, at_cols] = jnp.zeros(shape, BF)
            if ds == 0 or dr == 0:
                ref = ((rec_high, rec_low) if ds == 0 else (src_high, src_low))[ds + dr < 0]
                ref[...] = jnp.full(ref.shape, -1, jnp.int32)

    taps_table[...] = jnp.zeros(taps_table.shape, BF)
    for copy in fetch:
        copy.wait()
    for f in range(n_f):
        for c in range(2):
            first = (2 * f + c) * LANE
            taps_table[first : first + TAPS, :] = table[c, :, f, :].astype(BF)

    src_col[rows : 2 * rows, :] = columns_of(src_index[...])
    for t in range(tiles):
        rec_col[PAD + t * LANE : PAD + (t + 1) * LANE, :] = columns_of(
            rec_index[:, t * LANE : (t + 1) * LANE]
        )
    for z in range(DEPTHS):
        build_rec(z, range(counts[z]) if lefts[z] == 0 else range(1, counts[z] - 1))

    pl.semaphore_wait(barrier, along_src + (along_src + 1) * below_rec + n_freq - 1 - g)
    for number, way in enumerate(ways):
        if way[1] < 0:

            @pl.when(exists(way))
            def _(number=number, way=way):
                pl.semaphore_signal(
                    ready.at[number], inc=1, device_id=target(way), device_id_type=MESH
                )

    for d in range(1, n_freq):

        @pl.when(g + d < n_freq)
        def _(d=d):
            pl.semaphore_signal(
                peer_ready.at[d - 1], inc=1, device_id={"freq": g + d}, device_id_type=MESH
            )

    def send(f, number, way):
        if f == 0 and number < 4:
            index_copy(number, way).start()
        halo_copy(f, number, way).start()

    for f in range(n_f):
        for number, way in enumerate(ways):
            if way[1] <= 0:

                @pl.when(exists(way))
                def _(f=f, number=number, way=way):
                    send(f, number, way)


    for t in range(tiles):
        at = slice(t * LANE, (t + 1) * LANE)
        bins = offset_bin[:, at]
        for z in range(DEPTHS):
            line = jnp.concatenate(
                [bin_weight[z : z + 1, :], jnp.zeros((1, LANE - bin_weight.shape[1]), F32)], axis=1
            )
            spread = jnp.broadcast_to(line, (rows, LANE))
            weights[z, :, at] = jnp.take_along_axis(
                spread, bins, axis=1, mode="promise_in_bounds"
            )

    for f in range(n_f):
        for number, way in enumerate(ways):
            if way[1] > 0:

                @pl.when(exists(way))
                def _(f=f, number=number, way=way):
                    if f == 0:
                        back = ways.index((-way[0], -way[1]))
                        pl.semaphore_wait(ready.at[back], 1)
                    send(f, number, way)

    for number, way in enumerate(ways[:4]):

        @pl.when(exists((-way[0], -way[1])))
        def _(number=number, way=way):
            index_copy(number, way).wait_recv()

    src_col[:rows, :] = columns_of(src_low[...])
    src_col[2 * rows :, :] = columns_of(src_high[...])
    rec_col[:PAD, :] = columns_of(rec_low[...])
    rec_col[PAD + cols :, :] = columns_of(rec_high[...])
    for z in range(DEPTHS):
        if lefts[z]:
            build_rec(z, (0, counts[z] - 1))
        build_src(z)

    sends = []
    for f in range(n_f):
        own[f].wait()
        for number, way in enumerate(ways):

            @pl.when(exists((-way[0], -way[1])))
            def _(f=f, number=number, way=way):
                halo_copy(f, number, way).wait_recv()

        held = (x0.at[f], x1, x2)
        for z in range(DEPTHS):
            left = lefts[z]
            n_in, n_out = rows + 2 * left + 2 * HALF, rows + 2 * left
            source = held[z]
            for n in range(counts[z]):
                wide = 2 * LANE if (n + 2) * LANE <= source.shape[-1] else LANE
                window = source[:, :, n * LANE : n * LANE + wide].reshape(2 * n_in, wide)
                y = across(window, rec_op[f, starts[z] + n, :, :wide])
                at = slice(n * LANE, (n + 1) * LANE)
                q[0, :n_in, at] = (y[:n_in, :LANE] - y[n_in:, LANE:]).astype(BF)
                q[1, :n_in, at] = (y[:n_in, LANE:] + y[n_in:, :LANE]).astype(BF)
            op = (src_op0, src_op1, src_op2)[z][f, :, :n_in]
            reals = []
            for n in range(counts[z]):
                at = slice(n * LANE, (n + 1) * LANE)
                pair = jnp.concatenate([q[0, :n_in, at], q[1, :n_in, at]], axis=1)
                y = jnp.dot(op, pair, preferred_element_type=F32)
                real = (y[:n_out, :LANE] - y[n_out:, LANE:]).astype(BF)
                imag = (y[:n_out, LANE:] + y[n_out:, :LANE]).astype(BF)
                if z + 1 < DEPTHS:
                    held[z + 1][0, :, at] = real
                    held[z + 1][1, :, at] = imag
                else:
                    fin[0, f, :, at] = real
                    fin[1, f, :, at] = imag
                reals.append(real[left : left + rows, :].astype(F32))
            whole = jnp.concatenate(reals, axis=1) if left else None
            if left:
                whole = pltpu.roll(whole, whole.shape[1] - left, 1)
            for t in range(tiles):
                at = slice(t * LANE, (t + 1) * LANE)
                term = weights[z, :, at] * (whole[:, at] if left else reals[t])
                if z == 0 and f == 0:
                    part[:, at] = term
                elif z + 1 == DEPTHS and f == n_f - 1:
                    part_bf[:, at] = (part[:, at] + term).astype(BF)
                else:
                    part[:, at] = part[:, at] + term

    for d in range(1, n_freq):

        @pl.when(g >= d)
        def _(d=d):
            pl.semaphore_wait(peer_ready.at[d - 1], 1)

    piece = rows // n_freq
    for d in range(1, n_freq):
        to = lax.rem(g + d, n_freq)
        copy = pltpu.make_async_remote_copy(
            src_ref=part_bf.at[pl.ds(pl.multiple_of(to * piece, piece), piece)],
            dst_ref=parts_in.at[d - 1],
            send_sem=part_send.at[d - 1],
            recv_sem=part_recv.at[d - 1],
            device_id={"freq": to},
            device_id_type=MESH,
        )
        copy.start()
        sends.append(copy)
    part_own[...] = part_bf[pl.ds(pl.multiple_of(g * piece, piece), piece), :]
    for f in range(n_f):
        for number, way in enumerate(ways):

            @pl.when(exists(way))
            def _(f=f, number=number, way=way):
                if f == 0 and number < 4:
                    index_copy(number, way).wait_send()
                halo_copy(f, number, way).wait_send()

    for copy in sends:
        copy.wait()


def finish(scale, fin, part_own, parts_in, wave_out, image_out, image, sems):
    copies = [
        pltpu.make_async_copy(fin, wave_out, sems.at[0]),
        pltpu.make_async_copy(image, image_out, sems.at[1]),
    ]
    copies[0].start()
    total = part_own[...].astype(F32)
    for d in range(parts_in.shape[0]):
        total = total + parts_in[d].astype(F32)
    image[...] = total * scale
    copies[1].start()
    for copy in copies:
        copy.wait()


def shards(wave, tap_table, src_index, rec_index, offset_bin, bin_weight):
    n_src, n_rec, n_freq = (lax.axis_size(a) for a in ("src", "rec", "freq"))
    _, n_f, rows, cols = wave.shape
    scale = 1.0 / math.sqrt(n_f * n_freq * DEPTHS)
    tiles = cols // LANE
    piece = rows // n_freq
    outs = [rows + 2 * (HALO - HALF * (z + 1)) for z in range(DEPTHS)]
    vmem = pl.BlockSpec(memory_space=pltpu.VMEM)
    hbm = pl.BlockSpec(memory_space=pltpu.HBM)
    dma = pltpu.SemaphoreType.DMA
    operands = [
        pltpu.with_memory_space_constraint(x, pltpu.HBM)
        for x in (wave, jnp.transpose(tap_table, (0, 3, 2, 1)), src_index, rec_index, offset_bin, bin_weight)
    ]
    results = pl.pallas_call(
        functools.partial(kernel, (n_src, n_rec, n_freq)),
        out_shape=(
            pltpu.VMEM(wave.shape, BF),
            pltpu.VMEM((piece, cols), BF),
            pltpu.VMEM((n_freq - 1, piece, cols), BF),
        ),
        in_specs=[hbm] * 6,
        out_specs=(vmem, vmem, vmem),
        scratch_shapes=[
            pltpu.VMEM((2, TAPS, n_f, tap_table.shape[1]), F32),
            pltpu.VMEM(src_index.shape, jnp.int32),
            pltpu.VMEM(rec_index.shape, jnp.int32),
            pltpu.VMEM(offset_bin.shape, jnp.int32),
            pltpu.VMEM(bin_weight.shape, F32),
            dma((5,)),
            pltpu.VMEM((n_f, 2, rows + 2 * HALO, cols + 2 * PAD), BF),
            pltpu.VMEM((2, outs[0], cols + LANE), BF),
            pltpu.VMEM((2, outs[1], cols + LANE), BF),
            pltpu.VMEM((2, rows + 2 * HALO, cols + LANE), BF),
            pltpu.VMEM((DEPTHS, rows), jnp.int32),
            pltpu.VMEM((DEPTHS, rows), jnp.int32),
            pltpu.VMEM((DEPTHS, PAD), jnp.int32),
            pltpu.VMEM((DEPTHS, PAD), jnp.int32),
            pltpu.VMEM((3 * rows, DEPTHS), F32),
            pltpu.VMEM((cols + 2 * PAD, DEPTHS), F32),
            pltpu.VMEM((n_f * 2 * LANE, tap_table.shape[1]), BF),
            pltpu.VMEM((3 * tiles + 2, LANE, n_f * 2 * LANE), F32),
            pltpu.VMEM((n_f, 3 * tiles + 2, 2 * LANE, 2 * LANE), BF),
            pltpu.VMEM((n_f, 2 * outs[0], 2 * LANE), BF),
            pltpu.VMEM((n_f, 2 * outs[1], LANE), BF),
            pltpu.VMEM((n_f, 2 * outs[2], LANE), BF),
            pltpu.VMEM((DEPTHS, rows, cols), F32),
            pltpu.VMEM((rows, cols), F32),
            pltpu.VMEM((rows, cols), BF),
            dma((n_f,)),
            dma((n_f, 8)),
            dma((n_f, 8)),
            dma((4,)),
            dma((4,)),
            dma((n_freq - 1,)),
            dma((n_freq - 1,)),
            pltpu.SemaphoreType.REGULAR((8,)),
            pltpu.SemaphoreType.REGULAR((n_freq - 1,)),
        ],
        compiler_params=pltpu.CompilerParams(
            collective_id=0, has_side_effects=True, vmem_limit_bytes=40 * 1024 * 1024
        ),
    )(*operands)
    return pl.pallas_call(
        functools.partial(finish, scale),
        out_shape=(
            jax.ShapeDtypeStruct(wave.shape, BF),
            jax.ShapeDtypeStruct((piece, cols), F32),
        ),
        in_specs=[vmem] * 3,
        out_specs=(hbm, hbm),
        scratch_shapes=[pltpu.VMEM((piece, cols), F32), dma((2,))],
        compiler_params=pltpu.CompilerParams(vmem_limit_bytes=4 * 1024 * 1024),
    )(*[pltpu.with_memory_space_constraint(x, pltpu.VMEM) for x in results])


def solution(mesh):
    placed = (
        P(None, "freq", "src", "rec"),
        P(None, None, "freq", None),
        P(None, "src"),
        P(None, "rec"),
        P("src", "rec"),
        P(),
    )
    return jax.shard_map(
        shards,
        mesh=mesh,
        in_specs=placed,
        out_specs=(P(None, "freq", "src", "rec"), P(("src", "freq"), "rec")),
        check_vma=False,
    )
```

time: 36.4 us -> 28.5 us (0.78)
  the two profiles are of different devices: /device:TPU:1 before, /device:TPU:391 now
where the time goes in v2:
time: 28.5 us; the launch traced here: 28.3 us
  Pallas kernels  27.7 us (97%)
  between operations  0.64 us (2%)
    pallas_call x1, Pallas kernels, shards(): pl.pallas_call(functools.partial(kernel, (n_src, n_rec, n_freq)), out_sha...  27 us
    pallas_call x1, Pallas kernels, shards(): pl.pallas_call(functools.partial(finish, scale), out_shape=(jax.ShapeDtyp...  0.72 us

profile of v2, /device:TPU:391, one launch (start us, length us, event | category | flops | bytes accessed | tf_op | source)
XLA Modules:
  0.0 28.3 jit_solution(17120724561464513726)
XLA Ops:
  0.6 27.0 %shard_map.77 = (bf16[2,2,64,512]{3,2,1,0:T(8,128)(2,1)S(1)}, bf16[16,512]{1,0:T(8,128)(2,1)S(1)}, bf16[3,16,512]{2,1,0:T(8,128)(2,1)S(1)}) custom-call(bf16[2,2,64,512]{3,2,1,0:T(8,128)(2,1)} %wave.1, f32[2,33,2,64]{3,2,1,0:T(2,128)} %bitcast.1, s32[3,64]{1,0:T(4,128)} %src_index_in.1, s32[3,512]{1,0:T(4,128)} %rec_index_in.1, s32[64,512]{1,0:T(8,128)} %offset_bin_in.1, ...), custom_call_target="tpu_custom_call" | custom-call | tf_op jit(solution)/shard_map/pallas_call | solution.py:431
  27.6 0.7 %shard_map.78 = (bf16[2,2,64,512]{3,2,1,0:T(8,128)(2,1)}, f32[16,512]{1,0:T(8,128)}) custom-call(bf16[2,2,64,512]{3,2,1,0:T(8,128)(2,1)S(1)} %get-tuple-element.5.fin, bf16[16,512]{1,0:T(8,128)(2,1)S(1)} %get-tuple-element.6.part_own, bf16[3,16,512]{2,1,0:T(8,128)(2,1)S(1)} %get-tuple-element.7.parts_in), custom_call_target="tpu_custom_call" | custom-call | tf_op jit(solution)/shard_map/pallas_call | solution.py:480

commit v3 on v2

--- a/solution.py
+++ b/solution.py
@@ -111,19 +111,34 @@
             where["rec"] = j + way[1]
         return where
 
+    is_origin = (i == 0) & (j == 0) & (g == 0)
+    rank = jnp.where((i == 0) & (j == 0), lax.rem(g + n_freq - 1, n_freq), g)
+
+    def toward_first(way):
+        return (i + way[0] == 0) & (j + way[1] == 0) & (g == 0)
+
+    def greets(way):
+        side = exists(way) & jnp.logical_not(is_origin)
+        return side & toward_first(way) if way[1] < 0 else side
+
+    def greeted(way):
+        side = exists(way) & jnp.logical_not(toward_first(way))
+        return side & is_origin if way[1] > 0 else side
+
     barrier = pltpu.get_barrier_semaphore()
     for way in ways:
-        if way[1] >= 0:
-
-            @pl.when(exists(way))
-            def _(way=way):
-                pl.semaphore_signal(barrier, inc=1, device_id=target(way), device_id_type=MESH)
+
+        @pl.when(greets(way))
+        def _(way=way):
+            pl.semaphore_signal(barrier, inc=1, device_id=target(way), device_id_type=MESH)
 
     for d in range(1, n_freq):
 
-        @pl.when(g >= d)
+        @pl.when(rank + d < n_freq)
         def _(d=d):
-            pl.semaphore_signal(barrier, inc=1, device_id={"freq": g - d}, device_id_type=MESH)
+            pl.semaphore_signal(
+                barrier, inc=1, device_id={"freq": lax.rem(g + d, n_freq)}, device_id_type=MESH
+            )
 
     fetch = [
         pltpu.make_async_copy(source, dest, in_sem.at[k])
@@ -150,9 +165,6 @@
     for copy in own:
         copy.start()
 
-    along_src = (i > 0).astype(jnp.int32) + (i < n_src - 1).astype(jnp.int32)
-    below_rec = (j > 0).astype(jnp.int32)
-
     def halo_copy(f, number, way):
         ds, dr = way
         from_rows = [pl.ds(0, rows), pl.ds(rows - HALO, HALO), pl.ds(0, HALO)][ds]
@@ -216,6 +228,39 @@
                 if op.shape[2] > LANE:
                     op[f, c * n_out : (c + 1) * n_out, LANE:] = high
 
+    pl.semaphore_wait(barrier, sum(greeted(way).astype(jnp.int32) for way in ways) + rank)
+    for number, way in enumerate(ways):
+
+        @pl.when(greeted(way) & jnp.logical_not(greets(way)))
+        def _(number=number, way=way):
+            pl.semaphore_signal(
+                ready.at[number], inc=1, device_id=target(way), device_id_type=MESH
+            )
+
+    for d in range(1, n_freq):
+
+        @pl.when(rank >= d)
+        def _(d=d):
+            pl.semaphore_signal(
+                peer_ready.at[d - 1],
+                inc=1,
+                device_id={"freq": lax.rem(g + n_freq - d, n_freq)},
+                device_id_type=MESH,
+            )
+
+    def send(f, number, way):
+        if f == 0 and number < 4:
+            index_copy(number, way).start()
+        halo_copy(f, number, way).start()
+
+    for group in ((4, 6, 2), (0, 1, 3, 5, 7)):
+        for f in range(n_f):
+            for number in group:
+
+                @pl.when(greeted(ways[number]))
+                def _(f=f, number=number):
+                    send(f, number, ways[number])
+
     for way in ways:
 
         @pl.when(jnp.logical_not(exists(way)))
@@ -247,38 +292,6 @@
     for z in range(DEPTHS):
         build_rec(z, range(counts[z]) if lefts[z] == 0 else range(1, counts[z] - 1))
 
-    pl.semaphore_wait(barrier, along_src + (along_src + 1) * below_rec + n_freq - 1 - g)
-    for number, way in enumerate(ways):
-        if way[1] < 0:
-
-            @pl.when(exists(way))
-            def _(number=number, way=way):
-                pl.semaphore_signal(
-                    ready.at[number], inc=1, device_id=target(way), device_id_type=MESH
-                )
-
-    for d in range(1, n_freq):
-
-        @pl.when(g + d < n_freq)
-        def _(d=d):
-            pl.semaphore_signal(
-                peer_ready.at[d - 1], inc=1, device_id={"freq": g + d}, device_id_type=MESH
-            )
-
-    def send(f, number, way):
-        if f == 0 and number < 4:
-            index_copy(number, way).start()
-        halo_copy(f, number, way).start()
-
-    for f in range(n_f):
-        for number, way in enumerate(ways):
-            if way[1] <= 0:
-
-                @pl.when(exists(way))
-                def _(f=f, number=number, way=way):
-                    send(f, number, way)
-
-
     for t in range(tiles):
         at = slice(t * LANE, (t + 1) * LANE)
         bins = offset_bin[:, at]
@@ -291,16 +304,16 @@
                 spread, bins, axis=1, mode="promise_in_bounds"
             )
 
-    for f in range(n_f):
+    for down in (False, True):
         for number, way in enumerate(ways):
-            if way[1] > 0:
-
-                @pl.when(exists(way))
-                def _(f=f, number=number, way=way):
-                    if f == 0:
-                        back = ways.index((-way[0], -way[1]))
-                        pl.semaphore_wait(ready.at[back], 1)
-                    send(f, number, way)
+            if (way[1] > 0) != down and (not down or max(way) <= 0):
+
+                @pl.when(greets(way) & jnp.logical_not(greeted(way)))
+                def _(number=number, way=way):
+                    back = ways.index((-way[0], -way[1]))
+                    pl.semaphore_wait(ready.at[back], 1)
+                    for f in range(n_f):
+                        send(f, number, way)
 
     for number, way in enumerate(ways[:4]):
 
@@ -368,7 +381,7 @@
 
     for d in range(1, n_freq):
 
-        @pl.when(g >= d)
+        @pl.when(rank + d < n_freq)
         def _(d=d):
             pl.semaphore_wait(peer_ready.at[d - 1], 1)
 

time: 28.5 us -> 25.9 us (0.909)
  the two profiles are of different devices: /device:TPU:391 before, /device:TPU:1 now
where the time goes in v3:
time: 25.9 us; the launch traced here: 25.8 us
  Pallas kernels  25.1 us (97%)
  between operations  0.64 us (2%)
    pallas_call x1, Pallas kernels, shards(): pl.pallas_call(functools.partial(kernel, (n_src, n_rec, n_freq)), out_sha...  24.4 us
    pallas_call x1, Pallas kernels, shards(): pl.pallas_call(functools.partial(finish, scale), out_shape=(jax.ShapeDtyp...  0.72 us

profile of v3, /device:TPU:1, one launch (start us, length us, event | category | flops | bytes accessed | tf_op | source)
XLA Modules:
  0.0 25.8 jit_solution(2127127207271431486)
XLA Ops:
  0.6 24.4 %shard_map.77 = (bf16[2,2,64,512]{3,2,1,0:T(8,128)(2,1)S(1)}, bf16[16,512]{1,0:T(8,128)(2,1)S(1)}, bf16[3,16,512]{2,1,0:T(8,128)(2,1)S(1)}) custom-call(bf16[2,2,64,512]{3,2,1,0:T(8,128)(2,1)} %wave.1, f32[2,33,2,64]{3,2,1,0:T(2,128)} %bitcast.1, s32[3,64]{1,0:T(4,128)} %src_index_in.1, s32[3,512]{1,0:T(4,128)} %rec_index_in.1, s32[64,512]{1,0:T(8,128)} %offset_bin_in.1, ...), custom_call_target="tpu_custom_call" | custom-call | tf_op jit(solution)/shard_map/pallas_call | solution.py:444
  25.1 0.7 %shard_map.78 = (bf16[2,2,64,512]{3,2,1,0:T(8,128)(2,1)}, f32[16,512]{1,0:T(8,128)}) custom-call(bf16[2,2,64,512]{3,2,1,0:T(8,128)(2,1)S(1)} %get-tuple-element.5.fin, bf16[16,512]{1,0:T(8,128)(2,1)S(1)} %get-tuple-element.6.part_own, bf16[3,16,512]{2,1,0:T(8,128)(2,1)S(1)} %get-tuple-element.7.parts_in), custom_call_target="tpu_custom_call" | custom-call | tf_op jit(solution)/shard_map/pallas_call | solution.py:493

commit v4 on v3

--- a/solution.py
+++ b/solution.py
@@ -90,6 +90,8 @@
     part_recv,
     ready,
     peer_ready,
+    edges,
+    corners,
 ):
     n_src, n_rec, n_freq = sizes
     _, n_f, rows, cols = wave.shape
@@ -139,6 +141,29 @@
             pl.semaphore_signal(
                 barrier, inc=1, device_id={"freq": lax.rem(g + d, n_freq)}, device_id_type=MESH
             )
+
+    def open_up():
+        pl.semaphore_wait(barrier, sum(greeted(way).astype(jnp.int32) for way in ways) + rank)
+        for number, way in enumerate(ways):
+
+            @pl.when(greeted(way) & jnp.logical_not(greets(way)))
+            def _(number=number, way=way):
+                pl.semaphore_signal(
+                    ready.at[number], inc=1, device_id=target(way), device_id_type=MESH
+                )
+
+        for d in range(1, n_freq):
+
+            @pl.when(rank >= d)
+            def _(d=d):
+                pl.semaphore_signal(
+                    peer_ready.at[d - 1],
+                    inc=1,
+                    device_id={"freq": lax.rem(g + n_freq - d, n_freq)},
+                    device_id_type=MESH,
+                )
+
+    pl.when(is_origin)(open_up)
 
     fetch = [
         pltpu.make_async_copy(source, dest, in_sem.at[k])
@@ -167,13 +192,17 @@
 
     def halo_copy(f, number, way):
         ds, dr = way
-        from_rows = [pl.ds(0, rows), pl.ds(rows - HALO, HALO), pl.ds(0, HALO)][ds]
+        from_rows = [pl.ds(HALO, rows), pl.ds(rows, HALO), pl.ds(HALO, HALO)][ds]
         to_rows = [pl.ds(HALO, rows), pl.ds(0, HALO), pl.ds(HALO + rows, HALO)][ds]
-        from_cols = [pl.ds(0, cols), pl.ds(cols - PAD, PAD), pl.ds(0, PAD)][dr]
+        from_cols = [pl.ds(PAD, cols), pl.ds(cols, PAD), pl.ds(PAD, PAD)][dr]
         to_cols = [pl.ds(PAD, cols), pl.ds(0, PAD), pl.ds(PAD + cols, PAD)][dr]
+        source, dest = x0.at[f, :, from_rows, from_cols], x0.at[f, :, to_rows, to_cols]
+        if ds and dr:
+            source = edges.at[f, int(dr > 0), pl.ds(0 if ds < 0 else rows - HALO, HALO)]
+            dest = corners.at[f, number - 4]
         return pltpu.make_async_remote_copy(
-            src_ref=wave.at[:, f, from_rows, from_cols],
-            dst_ref=x0.at[f, :, to_rows, to_cols],
+            src_ref=source,
+            dst_ref=dest,
             send_sem=send_sem.at[f, number],
             recv_sem=recv_sem.at[f, number],
             device_id=target(way),
@@ -228,25 +257,17 @@
                 if op.shape[2] > LANE:
                     op[f, c * n_out : (c + 1) * n_out, LANE:] = high
 
-    pl.semaphore_wait(barrier, sum(greeted(way).astype(jnp.int32) for way in ways) + rank)
-    for number, way in enumerate(ways):
-
-        @pl.when(greeted(way) & jnp.logical_not(greets(way)))
-        def _(number=number, way=way):
-            pl.semaphore_signal(
-                ready.at[number], inc=1, device_id=target(way), device_id_type=MESH
+    half = LANE // 2
+    low_half = lax.broadcasted_iota(jnp.int32, (rows, LANE), 1) < half
+    for f in range(n_f):
+        own[f].wait()
+        for side, at in enumerate((PAD, cols)):
+            real, imag = (
+                x0[f, c, HALO : HALO + rows, at : at + LANE].astype(F32) for c in range(2)
             )
-
-    for d in range(1, n_freq):
-
-        @pl.when(rank >= d)
-        def _(d=d):
-            pl.semaphore_signal(
-                peer_ready.at[d - 1],
-                inc=1,
-                device_id={"freq": lax.rem(g + n_freq - d, n_freq)},
-                device_id_type=MESH,
-            )
+            keep = low_half if side == 0 else jnp.logical_not(low_half)
+            edges[f, side] = jnp.where(keep, real, pltpu.roll(imag, half, 1)).astype(BF)
+    pl.when(jnp.logical_not(is_origin))(open_up)
 
     def send(f, number, way):
         if f == 0 and number < 4:
@@ -291,6 +312,8 @@
         )
     for z in range(DEPTHS):
         build_rec(z, range(counts[z]) if lefts[z] == 0 else range(1, counts[z] - 1))
+        if lefts[z] == 0:
+            build_src(z)
 
     for t in range(tiles):
         at = slice(t * LANE, (t + 1) * LANE)
@@ -328,16 +351,21 @@
     for z in range(DEPTHS):
         if lefts[z]:
             build_rec(z, (0, counts[z] - 1))
-        build_src(z)
+            build_src(z)
 
     sends = []
     for f in range(n_f):
-        own[f].wait()
         for number, way in enumerate(ways):
 
             @pl.when(exists((-way[0], -way[1])))
             def _(f=f, number=number, way=way):
                 halo_copy(f, number, way).wait_recv()
+                if way[0] and way[1]:
+                    at_rows = [None, slice(0, HALO), slice(HALO + rows, None)][way[0]]
+                    at_cols = [None, slice(0, PAD), slice(PAD + cols, None)][way[1]]
+                    pair = corners[f, number - 4]
+                    x0[f, 0, at_rows, at_cols] = pair
+                    x0[f, 1, at_rows, at_cols] = pltpu.roll(pair.astype(F32), half, 1).astype(BF)
 
         held = (x0.at[f], x1, x2)
         for z in range(DEPTHS):
@@ -485,6 +513,8 @@
             dma((n_freq - 1,)),
             pltpu.SemaphoreType.REGULAR((8,)),
             pltpu.SemaphoreType.REGULAR((n_freq - 1,)),
+            pltpu.VMEM((n_f, 2, rows, LANE), BF),
+            pltpu.VMEM((n_f, 4, HALO, LANE), BF),
         ],
         compiler_params=pltpu.CompilerParams(
             collective_id=0, has_side_effects=True, vmem_limit_bytes=40 * 1024 * 1024

time: 25.9 us -> 25.9 us (level)
  no operation moved by 1% of the time
where the time goes in v4:
time: 25.9 us; the launch traced here: 25.8 us
  Pallas kernels  25.1 us (97%)
  between operations  0.64 us (2%)
    pallas_call x1, Pallas kernels, shards(): pl.pallas_call(functools.partial(kernel, (n_src, n_rec, n_freq)), out_sha...  24.4 us
    pallas_call x1, Pallas kernels, shards(): pl.pallas_call(functools.partial(finish, scale), out_shape=(jax.ShapeDtyp...  0.72 us

profile of v4, /device:TPU:1, one launch (start us, length us, event | category | flops | bytes accessed | tf_op | source)
XLA Modules:
  0.0 25.8 jit_solution(12933112632090122178)
XLA Ops:
  0.6 24.4 %shard_map.77 = (bf16[2,2,64,512]{3,2,1,0:T(8,128)(2,1)S(1)}, bf16[16,512]{1,0:T(8,128)(2,1)S(1)}, bf16[3,16,512]{2,1,0:T(8,128)(2,1)S(1)}) custom-call(bf16[2,2,64,512]{3,2,1,0:T(8,128)(2,1)} %wave.1, f32[2,33,2,64]{3,2,1,0:T(2,128)} %bitcast.1, s32[3,64]{1,0:T(4,128)} %src_index_in.1, s32[3,512]{1,0:T(4,128)} %rec_index_in.1, s32[64,512]{1,0:T(8,128)} %offset_bin_in.1, ...), custom_call_target="tpu_custom_call" | custom-call | tf_op jit(solution)/shard_map/pallas_call | solution.py:472
  25.0 0.7 %shard_map.78 = (bf16[2,2,64,512]{3,2,1,0:T(8,128)(2,1)}, f32[16,512]{1,0:T(8,128)}) custom-call(bf16[2,2,64,512]{3,2,1,0:T(8,128)(2,1)S(1)} %get-tuple-element.5.fin, bf16[16,512]{1,0:T(8,128)(2,1)S(1)} %get-tuple-element.6.part_own, bf16[3,16,512]{2,1,0:T(8,128)(2,1)S(1)} %get-tuple-element.7.parts_in), custom_call_target="tpu_custom_call" | custom-call | tf_op jit(solution)/shard_map/pallas_call | solution.py:523

commit v5 on v3

--- a/solution.py
+++ b/solution.py
@@ -386,7 +386,7 @@
             pl.semaphore_wait(peer_ready.at[d - 1], 1)
 
     piece = rows // n_freq
-    for d in range(1, n_freq):
+    for d in sorted(range(1, n_freq), key=lambda d: d != n_freq // 2):
         to = lax.rem(g + d, n_freq)
         copy = pltpu.make_async_remote_copy(
             src_ref=part_bf.at[pl.ds(pl.multiple_of(to * piece, piece), piece)],

time: 25.9 us -> 26 us (level)
  no operation moved by 1% of the time
where the time goes in v5:
time: 26 us; the launch traced here: 25.8 us
  Pallas kernels  25.2 us (97%)
  between operations  0.64 us (2%)
    pallas_call x1, Pallas kernels, shards(): pl.pallas_call(functools.partial(kernel, (n_src, n_rec, n_freq)), out_sha...  24.4 us
    pallas_call x1, Pallas kernels, shards(): pl.pallas_call(functools.partial(finish, scale), out_shape=(jax.ShapeDtyp...  0.72 us

profile of v5, /device:TPU:1, one launch (start us, length us, event | category | flops | bytes accessed | tf_op | source)
XLA Modules:
  0.0 25.8 jit_solution(16332010496308385340)
XLA Ops:
  0.6 24.4 %shard_map.77 = (bf16[2,2,64,512]{3,2,1,0:T(8,128)(2,1)S(1)}, bf16[16,512]{1,0:T(8,128)(2,1)S(1)}, bf16[3,16,512]{2,1,0:T(8,128)(2,1)S(1)}) custom-call(bf16[2,2,64,512]{3,2,1,0:T(8,128)(2,1)} %wave.1, f32[2,33,2,64]{3,2,1,0:T(2,128)} %bitcast.1, s32[3,64]{1,0:T(4,128)} %src_index_in.1, s32[3,512]{1,0:T(4,128)} %rec_index_in.1, s32[64,512]{1,0:T(8,128)} %offset_bin_in.1, ...), custom_call_target="tpu_custom_call" | custom-call | tf_op jit(solution)/shard_map/pallas_call | solution.py:444
  25.1 0.7 %shard_map.78 = (bf16[2,2,64,512]{3,2,1,0:T(8,128)(2,1)}, f32[16,512]{1,0:T(8,128)}) custom-call(bf16[2,2,64,512]{3,2,1,0:T(8,128)(2,1)S(1)} %get-tuple-element.5.fin, bf16[16,512]{1,0:T(8,128)(2,1)S(1)} %get-tuple-element.6.part_own, bf16[3,16,512]{2,1,0:T(8,128)(2,1)S(1)} %get-tuple-element.7.parts_in), custom_call_target="tpu_custom_call" | custom-call | tf_op jit(solution)/shard_map/pallas_call | solution.py:493
